TPU v7x, 32 devices: a whole 2x2x4 slice. The times are simulated.
32 devices in a mesh: node: 8 (over y, x, core), dev: 4 (over z).
Axes of the slice: x: 2, y: 2, z: 4, core: 2. Of those that a mesh axis runs over, the one named last changes fastest.
Arguments:
- tokens: bfloat16 [128, 4096], P('node', 'dev'), may hold values from -6 to 6
- routes: int32 [128, 8], P('node'), may hold values from 0 to 7, as said below
- gate_codes: int32 [128, 8], P('node'), may hold values from 1 to 65535
- w_gate: bfloat16 [8, 4096, 2048], P('node', None, 'dev'), may hold values from -0.09375 to 0.09375
- w_up: bfloat16 [8, 4096, 2048], P('node', None, 'dev'), may hold values from -0.09375 to 0.09375
- w_down: bfloat16 [8, 2048, 4096], P('node', 'dev'), may hold values from -0.125 to 0.125
- cotangent: bfloat16 [128, 4096], P('node', 'dev'), may hold values from -6 to 6
Outputs:
- layer_out: bfloat16 [128, 4096], P('node', 'dev')
- token_grad: bfloat16 [128, 4096], P('node', 'dev')
- down_grad: bfloat16 [8, 2048, 4096], P('node', 'dev')
Inputs may be any that keep to these rules, and one draw needn't show every extreme that they name: `routes`: each token names 8 different experts, taken from at most 4 groups of 4 consecutive experts. Among the 16 tokens of one block (one index of node), no expert is named by more than 16 tokens, and in every block some expert is named by exactly 16.
All inputs are finite; a program needn't handle non-finite values.
Results may differ from a plain program's by a relative error of at most 0.012.
Values may be sent and summed in bfloat16 or wider, within the bound.
A program may use at most 64 MiB of HBM per device.

v0:
```python
import jax
import jax.numpy as jnp
from jax import lax
from jax.sharding import PartitionSpec as P

TOP_GROUPS = 4
GROUP_SIZE = 4
exact_mode = lax.Precision.HIGHEST


def slot_layout(routes, gate_codes, experts, capacity):
    tokens_here = routes.shape[0]
    member = (routes[:, :, None] == jnp.arange(experts, dtype=jnp.int32)[None, None, :]).astype(
        jnp.float32
    )
    named_by = jnp.sum(member, axis=1)
    earlier = (jnp.arange(tokens_here)[:, None] > jnp.arange(tokens_here)[None, :]).astype(
        jnp.float32
    )
    before = jnp.dot(earlier, named_by, precision=exact_mode)
    placed = named_by[:, :, None] * (
        before[:, :, None] == jnp.arange(capacity).astype(jnp.float32)[None, None, :]
    ).astype(jnp.float32)
    weights = gate_codes.astype(jnp.float32) / 65536.0
    gating = jnp.sum(member * weights[:, :, None], axis=1)
    return (placed, gating)


def deliver(local_rows, build, fold, initial):
    whole_rows = lax.all_gather(local_rows, "dev", axis=1, tiled=True)
    arrived = lax.all_to_all(build(whole_rows), "node", split_axis=0, concat_axis=0, tiled=True)
    return fold(initial, arrived, 0)


def send_back(partial_value):
    shares = lax.psum_scatter(
        partial_value.astype(jnp.bfloat16), "dev", scatter_dimension=2, tiled=True
    )
    return lax.all_to_all(shares, "node", split_axis=0, concat_axis=0, tiled=True)


def on_device(tokens, routes, gate_codes, w_gate, w_up, w_down, cotangent):
    experts = lax.axis_size("node")
    groups = experts // GROUP_SIZE
    chosen_count = min(TOP_GROUPS, groups)
    capacity = tokens.shape[0] * chosen_count // groups
    placed, gating = slot_layout(routes, gate_codes, experts, capacity)
    place_low = placed.astype(jnp.bfloat16)
    weighted = placed * gating[:, :, None]
    gate_mat = w_gate[0]
    up_mat = w_up[0]
    down_mat = w_down[0]
    hidden_width = gate_mat.shape[1]

    def spread_tokens(payload):
        return jnp.einsum(
            "tep,tf->epf", place_low, payload, preferred_element_type=jnp.float32
        ).astype(jnp.bfloat16)

    def spread_cotangent(payload):
        return jnp.einsum(
            "tep,tf->epf", weighted, payload.astype(jnp.float32), precision=exact_mode
        ).astype(jnp.bfloat16)

    def project_in(totals, portion, offset):
        gate_next = jnp.einsum("epf,fh->eph", portion, gate_mat, preferred_element_type=jnp.float32)
        up_next = jnp.einsum("epf,fh->eph", portion, up_mat, preferred_element_type=jnp.float32)
        return (gate_next, up_next)

    empty_hidden = jnp.zeros((experts, capacity, hidden_width), jnp.float32)
    gate_pre, up_pre = deliver(tokens, spread_tokens, project_in, (empty_hidden, empty_hidden))
    squash = jax.nn.sigmoid(gate_pre)
    hidden = (gate_pre * squash * up_pre).astype(jnp.bfloat16)
    partial_value = jnp.einsum("eph,hf->epf", hidden, down_mat, preferred_element_type=jnp.float32)
    returned = send_back(partial_value)
    layer_out = jnp.einsum(
        "tep,epf->tf", weighted, returned.astype(jnp.float32), precision=exact_mode
    ).astype(jnp.bfloat16)

    def project_cotangent(totals, portion, offset):
        grad_next = jnp.einsum("epf,hf->eph", portion, down_mat, preferred_element_type=jnp.float32)
        block_grad = jnp.einsum("eph,epf->hf", hidden, portion, preferred_element_type=jnp.float32)
        return (grad_next, block_grad)

    empty_down = jnp.zeros((hidden_width, down_mat.shape[1]), jnp.float32)
    hidden_grad, down_total = deliver(
        cotangent, spread_cotangent, project_cotangent, (empty_hidden, empty_down)
    )
    gate_grad = (hidden_grad * up_pre * squash * (1.0 + gate_pre * (1.0 - squash))).astype(
        jnp.bfloat16
    )
    up_grad = (hidden_grad * gate_pre * squash).astype(jnp.bfloat16)
    partial_back = jnp.einsum(
        "eph,fh->epf", gate_grad, gate_mat, preferred_element_type=jnp.float32
    )
    partial_back = partial_back + jnp.einsum(
        "eph,fh->epf", up_grad, up_mat, preferred_element_type=jnp.float32
    )
    returned_back = send_back(partial_back)
    token_grad = jnp.einsum(
        "tep,epf->tf", placed, returned_back.astype(jnp.float32), precision=exact_mode
    ).astype(jnp.bfloat16)
    return (layer_out, token_grad, down_total.astype(jnp.bfloat16)[None])


def solution(mesh):
    in_specs = (
        P("node", "dev"),
        P("node", None),
        P("node", None),
        P("node", None, "dev"),
        P("node", None, "dev"),
        P("node", "dev", None),
        P("node", "dev"),
    )
    out_specs = (P("node", "dev"), P("node", "dev"), P("node", "dev", None))
    return jax.shard_map(
        on_device, mesh=mesh, in_specs=in_specs, out_specs=out_specs, check_vma=False
    )
```

profile of v0, /device:TPU:0, one launch (start us, length us, event | category | flops | bytes accessed | tf_op | source)
XLA Modules:
  0.0 132.5 jit_solution(16287439819941731388)
XLA Ops:
  7.2 0.7 convert_multiply_fusion
  7.9 0.7 select_reduce_fusion
  8.6 0.1 fusion.38
  8.7 15.3 %all_gather.6 = bf16[16,4096]{1,0:T(8,128)(2,1)S(1)} all-gather(bf16[16,1024]{1,0:T(8,128)(2,1)} %param.7), channel_id=1, replica_groups=mesh['node'=8,'dev'=4] {'dev'}, dimensions={1}, use_global_device_ids=true | all-gather | bytes 163840 | tf_op jit(solution)/shard_map/all_gather | solution.py:30
  24.0 1.5 %convolution_convert_fusion.2 = bf16[8,16,4096]{2,1,0:T(8,128)(2,1)} fusion(bf16[16,4096]{1,0:T(8,128)(2,1)S(1)} %all_gather.6, f32[16,8]{0,1:T(8,128)S(1)} %get-tuple-element.4, f32[16]{0:T(128)S(1)} %iota_convert_fusion, f32[16,8]{0,1:T(8,128)S(1)} %fusion.38), kind=kOutput, calls=%fused_computation.6 | convolution fusion | flops 17305600 | bytes 1180736 | tf_op jit(solution)/shard_map/tep,tf->epf/dot_general | solution.py:56
  25.5 3.7 %all-to-all-start = ((bf16[8,16,4096]{2,1,0:T(8,128)(2,1)}), bf16[8,16,4096]{2,1,0:T(8,128)(2,1)S(1)}, u32[]{:S(2)}, u32[]{:S(2)}) async-start(bf16[8,16,4096]{2,1,0:T(8,128)(2,1)} %convolution_convert_fusion.2), calls=%async_computation | async-start | bytes 2097152 | tf_op jit(solution)/shard_map/all_to_all | solution.py:31
  29.2 13.7 %all_gather.7 = bf16[16,4096]{1,0:T(8,128)(2,1)S(1)} all-gather(bf16[16,1024]{1,0:T(8,128)(2,1)} %param.13), channel_id=1, replica_groups=mesh['node'=8,'dev'=4] {'dev'}, dimensions={1}, use_global_device_ids=true | all-gather | bytes 163840 | tf_op jit(solution)/shard_map/all_gather | solution.py:30
  42.8 2.1 %convolution_convert_fusion = bf16[8,16,4096]{2,1,0:T(8,128)(2,1)} fusion(bf16[16,4096]{1,0:T(8,128)(2,1)S(1)} %all_gather.7, f32[16,8]{0,1:T(8,128)S(1)} %get-tuple-element.3, f32[16,8]{0,1:T(8,128)S(1)} %get-tuple-element.4, f32[16]{0:T(128)S(1)} %iota_convert_fusion, f32[16,8]{0,1:T(8,128)S(1)} %fusion.38), kind=kOutput, calls=%fused_computation.4 | convolution fusion | flops 101193728 | bytes 1181248 | tf_op jit(solution)/shard_map/tep,tf->epf/dot_general | solution.py:61
  44.9 0.0 all-to-all-done
  44.9 4.1 %all-to-all-start.2 = ((bf16[8,16,4096]{2,1,0:T(8,128)(2,1)}), bf16[8,16,4096]{2,1,0:T(8,128)(2,1)S(1)}, u32[]{:S(2)}, u32[]{:S(2)}) async-start(bf16[8,16,4096]{2,1,0:T(8,128)(2,1)} %convolution_convert_fusion), calls=%async_computation.3 | async-start | bytes 2097152 | tf_op jit(solution)/shard_map/all_to_all | solution.py:31
  49.0 0.0 reduce-scatter.3.cloned.1.call-start
  49.1 0.0 copy-start.2
  49.1 3.1 %fusion.10 = f32[8,16,512]{2,1,0:T(8,128)S(1)} fusion(bf16[8,16,4096]{2,1,0:T(8,128)(2,1)S(1)} %all-to-all-done, bf16[1,4096,512]{2,1,0:T(8,128)(2,1)} %param.10), kind=kOutput, calls=%fused_computation.15 | convolution fusion | flops 536870912 | bytes 5505024 | tf_op jit(solution)/shard_map/epf,fh->eph/dot_general | solution.py:66
  52.1 0.4 copy-done.2
  52.5 0.0 copy-start
  52.5 0.8 multiply_convert_fusion.2
  53.3 1.4 %copy-done = bf16[1,512,4096]{2,1,0:T(8,128)(2,1)S(1)} copy-done((bf16[1,512,4096]{2,1,0:T(8,128)(2,1)S(1)}, bf16[1,512,4096]{2,1,0:T(8,128)(2,1)}, u32[]{:S(2)}) %copy-start) | copy-done | bytes 4194328
  54.7 1.7 %convolution_convert_fusion.1 = bf16[8,16,4096]{2,1,0:T(8,128)(2,1)} fusion(bf16[8,16,512]{2,1,0:T(8,128)(2,1)S(1)} %get-tuple-element.5, bf16[1,512,4096]{2,1,0:T(8,128)(2,1)S(1)} %copy-done), kind=kOutput, calls=%fused_computation.5 | convolution fusion | flops 537395200 | bytes 5373952 | tf_op jit(solution)/shard_map/eph,hf->epf/dot_general | solution.py:74
  56.4 0.0 reduce-scatter.3.cloned.1.call-update
  56.5 0.0 reduce-scatter.5.cloned.1.call-start
  56.5 7.9 %all-to-all-done.2 = bf16[8,16,4096]{2,1,0:T(8,128)(2,1)S(1)} async-done(((bf16[8,16,4096]{2,1,0:T(8,128)(2,1)}), bf16[8,16,4096]{2,1,0:T(8,128)(2,1)S(1)}, u32[]{:S(2)}, u32[]{:S(2)}) %all-to-all-start.2) | async-done | bytes 1048608 | tf_op jit(solution)/shard_map/all_to_all | solution.py:31
  64.4 0.0 copy-start.1
  64.4 3.9 %fusion.2 = f32[8,16,512]{2,1,0:T(8,128)S(1)} fusion(bf16[8,16,4096]{2,1,0:T(8,128)(2,1)S(1)} %all-to-all-done.2, bf16[1,512,4096]{2,1,0:T(8,128)(2,1)} %param.12), kind=kOutput, calls=%fused_computation.7 | convolution fusion | flops 536870912 | bytes 5505024 | tf_op jit(solution)/shard_map/epf,hf->eph/dot_general | solution.py:81
  68.3 0.0 copy-start.3
  68.3 0.0 copy-done.1
  68.3 1.5 %fusion.8 = f32[8,16,4096]{2,1,0:T(8,128)S(1)} fusion(bf16[1,4096,512]{2,1,0:T(8,128)(2,1)S(1)} %copy-done.1, f32[8,16,512]{2,1,0:T(8,128)S(1)} %fusion.10, f32[8,16,512]{2,1,0:T(8,128)S(1)} %fusion.2, f32[8,16,512]{2,1,0:T(8,128)S(1)} %get-tuple-element.6), kind=kOutput, calls=%fused_computation.13 | convolution fusion | flops 537526272 | bytes 7077888 | tf_op jit(solution)/shard_map/eph,fh->epf/dot_general | solution.py:93
  69.8 0.7 copy-done.3
  70.5 2.5 %fusion.1 = bf16[8,16,4096]{2,1,0:T(8,128)(2,1)} fusion(f32[8,16,4096]{2,1,0:T(8,128)S(1)} %fusion.8, bf16[1,4096,512]{2,1,0:T(8,128)(2,1)S(1)} %copy-done.3, f32[8,16,512]{2,1,0:T(8,128)S(1)} %fusion.2, f32[8,16,512]{2,1,0:T(8,128)S(1)} %fusion.10), kind=kOutput, calls=%fused_computation.3 | convolution fusion | flops 538312704 | bytes 7864320 | tf_op jit(solution)/shard_map/eph,fh->epf/dot_general | solution.py:96
  73.0 0.0 reduce-scatter.5.cloned.1.call-update
  73.0 12.7 %reduce-scatter.3.cloned.1.call-done = bf16[8,16,1024]{2,1,0:T(8,128)(2,1)} async-done(((bf16[8,16,4096]{2,1,0:T(8,128)(2,1)}), bf16[8,16,1024]{2,1,0:T(8,128)(2,1)}) %reduce-scatter.3.cloned.1.call-update) | async-done | bytes 262160 | tf_op jit(solution)/shard_map/reduce_scatter | solution.py:36
  85.7 3.6 %all-to-all-start.1 = ((bf16[8,16,1024]{2,1,0:T(8,128)(2,1)}), bf16[8,16,1024]{2,1,0:T(8,128)(2,1)S(1)}, u32[]{:S(2)}, u32[]{:S(2)}) async-start(bf16[8,16,1024]{2,1,0:T(8,128)(2,1)} %reduce-scatter.3.cloned.1.call-done), calls=%async_computation.2 | async-start | bytes 524288 | tf_op jit(solution)/shard_map/all_to_all | solution.py:39
  89.3 3.3 %fusion = bf16[1,512,4096]{2,1,0:T(8,128)(2,1)} fusion(bf16[8,16,512]{2,1,0:T(8,128)(2,1)S(1)} %get-tuple-element.5, bf16[8,16,4096]{2,1,0:T(8,128)(2,1)S(1)} %all-to-all-done.2), kind=kOutput, calls=%fused_computation.1 | convolution fusion | flops 538968064 | bytes 5373952 | tf_op jit(solution)/shard_map/eph,epf->hf/dot_general | solution.py:82
  92.6 21.3 %reduce-scatter.5.cloned.1.call-done = bf16[8,16,1024]{2,1,0:T(8,128)(2,1)} async-done(((bf16[8,16,4096]{2,1,0:T(8,128)(2,1)}), bf16[8,16,1024]{2,1,0:T(8,128)(2,1)}) %reduce-scatter.5.cloned.1.call-update) | async-done | bytes 262160 | tf_op jit(solution)/shard_map/reduce_scatter | solution.py:36
  113.9 0.0 all-to-all-done.1
  113.9 3.6 %all-to-all-start.3 = ((bf16[8,16,1024]{2,1,0:T(8,128)(2,1)}), bf16[8,16,1024]{2,1,0:T(8,128)(2,1)S(1)}, u32[]{:S(2)}, u32[]{:S(2)}) async-start(bf16[8,16,1024]{2,1,0:T(8,128)(2,1)} %reduce-scatter.5.cloned.1.call-done), calls=%async_computation.5 | async-start | bytes 524288 | tf_op jit(solution)/shard_map/all_to_all | solution.py:39
  117.6 1.1 fusion.12
  118.7 5.8 %all-to-all-done.3 = bf16[8,16,1024]{2,1,0:T(8,128)(2,1)S(1)} async-done(((bf16[8,16,1024]{2,1,0:T(8,128)(2,1)}), bf16[8,16,1024]{2,1,0:T(8,128)(2,1)S(1)}, u32[]{:S(2)}, u32[]{:S(2)}) %all-to-all-start.3) | async-done | bytes 262176 | tf_op jit(solution)/shard_map/all_to_all | solution.py:39
  124.5 1.1 fusion.13
  (1 shorter events, 0.0 us)
Async XLA Ops:
  25.5 19.5 %all-to-all-start = ((bf16[8,16,4096]{2,1,0:T(8,128)(2,1)}), bf16[8,16,4096]{2,1,0:T(8,128)(2,1)S(1)}, u32[]{:S(2)}, u32[]{:S(2)}) async-start(bf16[8,16,4096]{2,1,0:T(8,128)(2,1)} %convolution_convert_fusion.2), calls=%async_computation | async-start | bytes 2097152 | tf_op jit(solution)/shard_map/all_to_all | solution.py:31
  44.9 19.5 %all-to-all-start.2 = ((bf16[8,16,4096]{2,1,0:T(8,128)(2,1)}), bf16[8,16,4096]{2,1,0:T(8,128)(2,1)S(1)}, u32[]{:S(2)}, u32[]{:S(2)}) async-start(bf16[8,16,4096]{2,1,0:T(8,128)(2,1)} %convolution_convert_fusion), calls=%async_computation.3 | async-start | bytes 2097152 | tf_op jit(solution)/shard_map/all_to_all | solution.py:31
  49.0 36.7 %reduce-scatter.3.cloned.1.call-start = ((), (), s32[]{:S(2)}) async-start(), calls=%async_computation.6 | async-start | bytes 1310720 | tf_op jit(solution)/shard_map/reduce_scatter | solution.py:36
  49.1 3.5 %copy-start.2 = (bf16[1,4096,512]{2,1,0:T(8,128)(2,1)S(1)}, bf16[1,4096,512]{2,1,0:T(8,128)(2,1)}, u32[]{:S(2)}) copy-start(bf16[1,4096,512]{2,1,0:T(8,128)(2,1)} %param.11) | copy-start | bytes 12582916
  52.5 2.2 %copy-start = (bf16[1,512,4096]{2,1,0:T(8,128)(2,1)S(1)}, bf16[1,512,4096]{2,1,0:T(8,128)(2,1)}, u32[]{:S(2)}) copy-start(bf16[1,512,4096]{2,1,0:T(8,128)(2,1)} %param.12) | copy-start | bytes 12582916
  56.5 57.5 %reduce-scatter.5.cloned.1.call-start = ((), (), s32[]{:S(2)}) async-start(), calls=%async_computation.7 | async-start | bytes 1310720 | tf_op jit(solution)/shard_map/reduce_scatter | solution.py:36
  64.4 3.9 %copy-start.1 = (bf16[1,4096,512]{2,1,0:T(8,128)(2,1)S(1)}, bf16[1,4096,512]{2,1,0:T(8,128)(2,1)}, u32[]{:S(2)}) copy-start(bf16[1,4096,512]{2,1,0:T(8,128)(2,1)} %param.10) | copy-start | bytes 12582916
  68.3 2.2 %copy-start.3 = (bf16[1,4096,512]{2,1,0:T(8,128)(2,1)S(1)}, bf16[1,4096,512]{2,1,0:T(8,128)(2,1)}, u32[]{:S(2)}) copy-start(bf16[1,4096,512]{2,1,0:T(8,128)(2,1)} %param.11) | copy-start | bytes 12582916
  85.7 28.2 %all-to-all-start.1 = ((bf16[8,16,1024]{2,1,0:T(8,128)(2,1)}), bf16[8,16,1024]{2,1,0:T(8,128)(2,1)S(1)}, u32[]{:S(2)}, u32[]{:S(2)}) async-start(bf16[8,16,1024]{2,1,0:T(8,128)(2,1)} %reduce-scatter.3.cloned.1.call-done), calls=%async_computation.2 | async-start | bytes 524288 | tf_op jit(solution)/shard_map/all_to_all | solution.py:39
  113.9 10.6 %all-to-all-start.3 = ((bf16[8,16,1024]{2,1,0:T(8,128)(2,1)}), bf16[8,16,1024]{2,1,0:T(8,128)(2,1)S(1)}, u32[]{:S(2)}, u32[]{:S(2)}) async-start(bf16[8,16,1024]{2,1,0:T(8,128)(2,1)} %reduce-scatter.5.cloned.1.call-done), calls=%async_computation.5 | async-start | bytes 524288 | tf_op jit(solution)/shard_map/all_to_all | solution.py:39
Sparse Core Ops, SparseCore 0:
  56.6 29.0 reduce-scatter.2
  88.1 25.7 reduce-scatter.4
where the time goes:
time: 133 us; the launch traced here: 132 us
  waiting for transfers between devices  47.7 us (36%)
  blocking collectives  28.9 us (22%)
  matrix products  22.7 us (17%)
  starting transfers between devices  15.2 us (11%)
  between operations  14.1 us (11%)
  local copies, waits for them, and re-layouts  2.48 us (2%)
  other arithmetic  1.4 us (1%)
    reduce_scatter x2, waiting for transfers between devices, send_back(): lax.psum_scatter(partial_value.astype(jnp.bfloat16), 'dev', scatter_dimen...  34 us
    all_gather x2, blocking collectives, deliver(): whole_rows = lax.all_gather(local_rows, 'dev', axis=1, tiled=True)  28.9 us
    all_to_all x2, waiting for transfers between devices, deliver(): lax.all_to_all(build(whole_rows), 'node', split_axis=0, concat_axis=0, ti...  7.91 us
    all_to_all x2, starting transfers between devices, deliver(): lax.all_to_all(build(whole_rows), 'node', split_axis=0, concat_axis=0, ti...  7.81 us
    all_to_all x2, starting transfers between devices, send_back(): lax.all_to_all(shares, 'node', split_axis=0, concat_axis=0, tiled=True)  7.29 us
    all_to_all x2, waiting for transfers between devices, send_back(): lax.all_to_all(shares, 'node', split_axis=0, concat_axis=0, tiled=True)  5.79 us
    dot_general x1, matrix products, project_cotangent(): jnp.einsum('epf,hf->eph', portion, down_mat, preferred_element_type=jnp.f...  3.88 us
    dot_general x1, matrix products, project_cotangent(): jnp.einsum('eph,epf->hf', hidden, portion, preferred_element_type=jnp.flo...  3.29 us
  transfers between devices with their start and end apart: 6, of which 4 were waited for; matrix products, arithmetic and copies ran while one was open for 15% of the time, Pallas kernels for 0%

commit v1 on v0

--- a/solution.py
+++ b/solution.py
@@ -27,7 +27,12 @@
 
 
 def deliver(local_rows, build, fold, initial):
-    whole_rows = lax.all_gather(local_rows, "dev", axis=1, tiled=True)
+    ring = [local_rows]
+    for hop in range(3):
+        ring.append(lax.ppermute(ring[-1], "dev", [(dev, (dev + 1) % 4) for dev in range(4)]))
+    whole_rows = jnp.roll(
+        jnp.concatenate(ring[::-1], axis=1), (lax.axis_index("dev") + 1) * ring[0].shape[1], axis=1
+    )
     arrived = lax.all_to_all(build(whole_rows), "node", split_axis=0, concat_axis=0, tiled=True)
     return fold(initial, arrived, 0)
 

time: 133 us -> 138 us (1.038)
  blocking collectives: 28.9 us -> 0 us
  waiting for transfers between devices: 47.7 us -> 75.8 us
  starting transfers between devices: 15.2 us -> 18.6 us
  matrix products: 22.7 us -> 24.8 us
    ppermute x0 -> x6, waiting for transfers between devices: none -> 31.4 us  [deliver(): lax.ppermute(ring[-1], 'dev', [(dev, (dev + 1) % 4) for dev in range(4)])]
    all_gather x2 -> x0, blocking collectives: 28.9 us -> none  [deliver(): whole_rows = lax.all_gather(local_rows, 'dev', axis=1, tiled=True)]
    reduce_scatter x2, waiting for transfers between devices: 34 us -> 30.6 us  [send_back(): lax.psum_scatter(partial_value.astype(jnp.bfloat16), 'dev', scatter_dimen...]
    ppermute x0 -> x6, starting transfers between devices: none -> 3.09 us  [deliver(): lax.ppermute(ring[-1], 'dev', [(dev, (dev + 1) % 4) for dev in range(4)])]
  transfers between devices with their start and end apart: 6 -> 12, of which waited for: 4 -> 10; matrix products, arithmetic and copies ran while one was open for 15% -> 16% of each run, Pallas kernels for 0% -> 0%
where the time goes in v1:
time: 138 us; the launch traced here: 137 us
  waiting for transfers between devices  75.8 us (55%)
  matrix products  24.8 us (18%)
  starting transfers between devices  18.6 us (13%)
  between operations  14.1 us (10%)
  local copies, waits for them, and re-layouts  2.49 us (2%)
  other arithmetic  1.39 us (1%)
    ppermute x6, waiting for transfers between devices, deliver(): lax.ppermute(ring[-1], 'dev', [(dev, (dev + 1) % 4) for dev in range(4)])  31.4 us
    reduce_scatter x2, waiting for transfers between devices, send_back(): lax.psum_scatter(partial_value.astype(jnp.bfloat16), 'dev', scatter_dimen...  30.6 us
    all_to_all x2, starting transfers between devices, deliver(): lax.all_to_all(build(whole_rows), 'node', split_axis=0, concat_axis=0, ti...  8.13 us
    all_to_all x2, waiting for transfers between devices, deliver(): lax.all_to_all(build(whole_rows), 'node', split_axis=0, concat_axis=0, ti...  7.92 us
    all_to_all x2, starting transfers between devices, send_back(): lax.all_to_all(shares, 'node', split_axis=0, concat_axis=0, tiled=True)  7.32 us
    all_to_all x2, waiting for transfers between devices, send_back(): lax.all_to_all(shares, 'node', split_axis=0, concat_axis=0, tiled=True)  5.79 us
    dot_general x1, matrix products, project_cotangent(): jnp.einsum('epf,hf->eph', portion, down_mat, preferred_element_type=jnp.f...  3.86 us
    dot_general x1, matrix products, project_cotangent(): jnp.einsum('eph,epf->hf', hidden, portion, preferred_element_type=jnp.flo...  3.29 us
  transfers between devices with their start and end apart: 12, of which 10 were waited for; matrix products, arithmetic and copies ran while one was open for 16% of the time, Pallas kernels for 0%

profile of v1, /device:TPU:0, one launch (start us, length us, event | category | flops | bytes accessed | tf_op | source)
XLA Modules:
  0.0 137.2 jit_solution(14461652059188065462)
XLA Ops:
  7.2 3.1 %collective-permute-start = (bf16[16,1024]{1,0:T(8,128)(2,1)}, bf16[16,1024]{1,0:T(8,128)(2,1)S(1)}, u32[]{:S(2)}, u32[]{:S(2)}) collective-permute-start(bf16[16,1024]{1,0:T(8,128)(2,1)} %param.9), channel_id=1, source_target_pairs={{0,1},{1,2},{2,3},{3,0},{4,5},{5,6},{6,7},{7,4},{8,9},{9,10},{10,1... | collective-permute-start | bytes 98312 | tf_op jit(solution)/shard_map/ppermute | solution.py:32
  10.2 0.7 convert_multiply_fusion
  10.9 0.7 select_reduce_fusion
  11.6 2.7 %collective-permute-done = bf16[16,1024]{1,0:T(8,128)(2,1)S(1)} collective-permute-done((bf16[16,1024]{1,0:T(8,128)(2,1)}, bf16[16,1024]{1,0:T(8,128)(2,1)S(1)}, u32[]{:S(2)}, u32[]{:S(2)}) %collective-permute-start) | collective-permute-done | bytes 32800 | tf_op jit(solution)/shard_map/ppermute | solution.py:32
  14.4 0.0 collective-permute-start.1
  14.4 0.1 fusion.56
  14.5 5.6 %collective-permute-done.1 = bf16[16,1024]{1,0:T(8,128)(2,1)S(1)} collective-permute-done((bf16[16,1024]{1,0:T(8,128)(2,1)S(1)}, bf16[16,1024]{1,0:T(8,128)(2,1)S(1)}, u32[]{:S(2)}, u32[]{:S(2)}) %collective-permute-start.1) | collective-permute-done | bytes 32800 | tf_op jit(solution)/shard_map/ppermute | solution.py:32
  20.1 0.0 collective-permute-start.2
  20.1 5.7 %collective-permute-done.2 = bf16[16,1024]{1,0:T(8,128)(2,1)S(1)} collective-permute-done((bf16[16,1024]{1,0:T(8,128)(2,1)S(1)}, bf16[16,1024]{1,0:T(8,128)(2,1)S(1)}, u32[]{:S(2)}, u32[]{:S(2)}) %collective-permute-start.2) | collective-permute-done | bytes 32800 | tf_op jit(solution)/shard_map/ppermute | solution.py:32
  25.8 2.6 %convolution_convert_fusion.2 = bf16[8,16,4096]{2,1,0:T(8,128)(2,1)} fusion(s32[]{:T(128)S(6)} %select_n.13, bf16[16,1024]{1,0:T(8,128)(2,1)S(1)} %collective-permute-done.2, bf16[16,1024]{1,0:T(8,128)(2,1)S(1)} %collective-permute-done.1, bf16[16,1024]{1,0:T(8,128)(2,1)S(1)} %collective-permute-done, bf16[16,1024]{1,0:T(8,128)(2,1)} %param.9, ...), kind=kOutput, calls=%fused_computation.6 | convolution fusion | flops 18354176 | bytes 1180740 | tf_op jit(solution)/shard_map/tep,tf->epf/dot_general | solution.py:61
  28.4 3.9 %all-to-all-start = ((bf16[8,16,4096]{2,1,0:T(8,128)(2,1)}), bf16[8,16,4096]{2,1,0:T(8,128)(2,1)S(1)}, u32[]{:S(2)}, u32[]{:S(2)}) async-start(bf16[8,16,4096]{2,1,0:T(8,128)(2,1)} %convolution_convert_fusion.2), calls=%async_computation | async-start | bytes 2097152 | tf_op jit(solution)/shard_map/all_to_all | solution.py:36
  32.3 0.0 collective-permute-start.3
  32.3 5.9 %collective-permute-done.3 = bf16[16,1024]{1,0:T(8,128)(2,1)S(1)} collective-permute-done((bf16[16,1024]{1,0:T(8,128)(2,1)}, bf16[16,1024]{1,0:T(8,128)(2,1)S(1)}, u32[]{:S(2)}, u32[]{:S(2)}) %collective-permute-start.3) | collective-permute-done | bytes 32800 | tf_op jit(solution)/shard_map/ppermute | solution.py:32
  38.2 0.0 collective-permute-start.4
  38.2 5.7 %collective-permute-done.4 = bf16[16,1024]{1,0:T(8,128)(2,1)S(1)} collective-permute-done((bf16[16,1024]{1,0:T(8,128)(2,1)S(1)}, bf16[16,1024]{1,0:T(8,128)(2,1)S(1)}, u32[]{:S(2)}, u32[]{:S(2)}) %collective-permute-start.4) | collective-permute-done | bytes 32800 | tf_op jit(solution)/shard_map/ppermute | solution.py:32
  43.9 0.0 collective-permute-start.5
  43.9 5.7 %collective-permute-done.5 = bf16[16,1024]{1,0:T(8,128)(2,1)S(1)} collective-permute-done((bf16[16,1024]{1,0:T(8,128)(2,1)S(1)}, bf16[16,1024]{1,0:T(8,128)(2,1)S(1)}, u32[]{:S(2)}, u32[]{:S(2)}) %collective-permute-start.5) | collective-permute-done | bytes 32800 | tf_op jit(solution)/shard_map/ppermute | solution.py:32
  49.7 3.1 %convolution_convert_fusion = bf16[8,16,4096]{2,1,0:T(8,128)(2,1)} fusion(s32[]{:T(128)S(6)} %select_n.13, bf16[16,1024]{1,0:T(8,128)(2,1)S(1)} %collective-permute-done.5, bf16[16,1024]{1,0:T(8,128)(2,1)S(1)} %collective-permute-done.4, bf16[16,1024]{1,0:T(8,128)(2,1)S(1)} %collective-permute-done.3, bf16[16,1024]{1,0:T(8,128)(2,1)} %param.15, ...), kind=kOutput, calls=%fused_computation.4 | convolution fusion | flops 102242304 | bytes 1181252 | tf_op jit(solution)/shard_map/tep,tf->epf/dot_general | solution.py:66
  52.8 0.0 all-to-all-done
  52.8 4.2 %all-to-all-start.2 = ((bf16[8,16,4096]{2,1,0:T(8,128)(2,1)}), bf16[8,16,4096]{2,1,0:T(8,128)(2,1)S(1)}, u32[]{:S(2)}, u32[]{:S(2)}) async-start(bf16[8,16,4096]{2,1,0:T(8,128)(2,1)} %convolution_convert_fusion), calls=%async_computation.3 | async-start | bytes 2097152 | tf_op jit(solution)/shard_map/all_to_all | solution.py:36
  57.0 0.0 reduce-scatter.3.cloned.1.call-start
  57.0 0.0 copy-start.2
  57.1 3.1 %fusion.10 = f32[8,16,512]{2,1,0:T(8,128)S(1)} fusion(bf16[8,16,4096]{2,1,0:T(8,128)(2,1)S(1)} %all-to-all-done, bf16[1,4096,512]{2,1,0:T(8,128)(2,1)} %param.12), kind=kOutput, calls=%fused_computation.15 | convolution fusion | flops 536870912 | bytes 5505024 | tf_op jit(solution)/shard_map/epf,fh->eph/dot_general | solution.py:71
  60.1 0.4 copy-done.2
  60.5 0.0 copy-start
  60.5 0.8 multiply_convert_fusion.2
  61.3 1.4 %copy-done = bf16[1,512,4096]{2,1,0:T(8,128)(2,1)S(1)} copy-done((bf16[1,512,4096]{2,1,0:T(8,128)(2,1)S(1)}, bf16[1,512,4096]{2,1,0:T(8,128)(2,1)}, u32[]{:S(2)}) %copy-start) | copy-done | bytes 4194328
  62.7 1.7 %convolution_convert_fusion.1 = bf16[8,16,4096]{2,1,0:T(8,128)(2,1)} fusion(bf16[8,16,512]{2,1,0:T(8,128)(2,1)S(1)} %get-tuple-element.6, bf16[1,512,4096]{2,1,0:T(8,128)(2,1)S(1)} %copy-done), kind=kOutput, calls=%fused_computation.5 | convolution fusion | flops 537395200 | bytes 5373952 | tf_op jit(solution)/shard_map/eph,hf->epf/dot_general | solution.py:79
  64.4 0.0 reduce-scatter.3.cloned.1.call-update
  64.4 0.0 reduce-scatter.5.cloned.1.call-start
  64.5 7.9 %all-to-all-done.2 = bf16[8,16,4096]{2,1,0:T(8,128)(2,1)S(1)} async-done(((bf16[8,16,4096]{2,1,0:T(8,128)(2,1)}), bf16[8,16,4096]{2,1,0:T(8,128)(2,1)S(1)}, u32[]{:S(2)}, u32[]{:S(2)}) %all-to-all-start.2) | async-done | bytes 1048608 | tf_op jit(solution)/shard_map/all_to_all | solution.py:36
  72.4 0.0 copy-start.1
  72.4 3.9 %fusion.2 = f32[8,16,512]{2,1,0:T(8,128)S(1)} fusion(bf16[8,16,4096]{2,1,0:T(8,128)(2,1)S(1)} %all-to-all-done.2, bf16[1,512,4096]{2,1,0:T(8,128)(2,1)} %param.14), kind=kOutput, calls=%fused_computation.7 | convolution fusion | flops 536870912 | bytes 5505024 | tf_op jit(solution)/shard_map/epf,hf->eph/dot_general | solution.py:86
  76.3 0.0 copy-start.3
  76.3 0.0 copy-done.1
  76.3 1.5 %fusion.8 = f32[8,16,4096]{2,1,0:T(8,128)S(1)} fusion(bf16[1,4096,512]{2,1,0:T(8,128)(2,1)S(1)} %copy-done.1, f32[8,16,512]{2,1,0:T(8,128)S(1)} %fusion.10, f32[8,16,512]{2,1,0:T(8,128)S(1)} %fusion.2, f32[8,16,512]{2,1,0:T(8,128)S(1)} %get-tuple-element.7), kind=kOutput, calls=%fused_computation.13 | convolution fusion | flops 537526272 | bytes 7077888 | tf_op jit(solution)/shard_map/eph,fh->epf/dot_general | solution.py:98
  77.8 0.7 copy-done.3
  78.5 2.5 %fusion.1 = bf16[8,16,4096]{2,1,0:T(8,128)(2,1)} fusion(f32[8,16,4096]{2,1,0:T(8,128)S(1)} %fusion.8, bf16[1,4096,512]{2,1,0:T(8,128)(2,1)S(1)} %copy-done.3, f32[8,16,512]{2,1,0:T(8,128)S(1)} %fusion.2, f32[8,16,512]{2,1,0:T(8,128)S(1)} %fusion.10), kind=kOutput, calls=%fused_computation.3 | convolution fusion | flops 538312704 | bytes 7864320 | tf_op jit(solution)/shard_map/eph,fh->epf/dot_general | solution.py:101
  81.0 0.0 reduce-scatter.5.cloned.1.call-update
  81.0 9.4 %reduce-scatter.3.cloned.1.call-done = bf16[8,16,1024]{2,1,0:T(8,128)(2,1)} async-done(((bf16[8,16,4096]{2,1,0:T(8,128)(2,1)}), bf16[8,16,1024]{2,1,0:T(8,128)(2,1)}) %reduce-scatter.3.cloned.1.call-update) | async-done | bytes 262160 | tf_op jit(solution)/shard_map/reduce_scatter | solution.py:41
  90.4 3.7 %all-to-all-start.1 = ((bf16[8,16,1024]{2,1,0:T(8,128)(2,1)}), bf16[8,16,1024]{2,1,0:T(8,128)(2,1)S(1)}, u32[]{:S(2)}, u32[]{:S(2)}) async-start(bf16[8,16,1024]{2,1,0:T(8,128)(2,1)} %reduce-scatter.3.cloned.1.call-done), calls=%async_computation.2 | async-start | bytes 524288 | tf_op jit(solution)/shard_map/all_to_all | solution.py:44
  94.1 3.3 %fusion = bf16[1,512,4096]{2,1,0:T(8,128)(2,1)} fusion(bf16[8,16,512]{2,1,0:T(8,128)(2,1)S(1)} %get-tuple-element.6, bf16[8,16,4096]{2,1,0:T(8,128)(2,1)S(1)} %all-to-all-done.2), kind=kOutput, calls=%fused_computation.1 | convolution fusion | flops 538968064 | bytes 5373952 | tf_op jit(solution)/shard_map/eph,epf->hf/dot_general | solution.py:87
  97.3 21.2 %reduce-scatter.5.cloned.1.call-done = bf16[8,16,1024]{2,1,0:T(8,128)(2,1)} async-done(((bf16[8,16,4096]{2,1,0:T(8,128)(2,1)}), bf16[8,16,1024]{2,1,0:T(8,128)(2,1)}) %reduce-scatter.5.cloned.1.call-update) | async-done | bytes 262160 | tf_op jit(solution)/shard_map/reduce_scatter | solution.py:41
  118.6 0.0 all-to-all-done.1
  118.6 3.7 %all-to-all-start.3 = ((bf16[8,16,1024]{2,1,0:T(8,128)(2,1)}), bf16[8,16,1024]{2,1,0:T(8,128)(2,1)S(1)}, u32[]{:S(2)}, u32[]{:S(2)}) async-start(bf16[8,16,1024]{2,1,0:T(8,128)(2,1)} %reduce-scatter.5.cloned.1.call-done), calls=%async_computation.5 | async-start | bytes 524288 | tf_op jit(solution)/shard_map/all_to_all | solution.py:44
  122.3 1.1 fusion.12
  123.4 5.8 %all-to-all-done.3 = bf16[8,16,1024]{2,1,0:T(8,128)(2,1)S(1)} async-done(((bf16[8,16,1024]{2,1,0:T(8,128)(2,1)}), bf16[8,16,1024]{2,1,0:T(8,128)(2,1)S(1)}, u32[]{:S(2)}, u32[]{:S(2)}) %all-to-all-start.3) | async-done | bytes 262176 | tf_op jit(solution)/shard_map/all_to_all | solution.py:44
  129.2 1.1 fusion.13
  (1 shorter events, 0.0 us)
Async XLA Ops:
  7.2 7.2 %collective-permute-start = (bf16[16,1024]{1,0:T(8,128)(2,1)}, bf16[16,1024]{1,0:T(8,128)(2,1)S(1)}, u32[]{:S(2)}, u32[]{:S(2)}) collective-permute-start(bf16[16,1024]{1,0:T(8,128)(2,1)} %param.9), channel_id=1, source_target_pairs={{0,1},{1,2},{2,3},{3,0},{4,5},{5,6},{6,7},{7,4},{8,9},{9,10},{10,1... | collective-permute-start | bytes 98312 | tf_op jit(solution)/shard_map/ppermute | solution.py:32
  14.4 5.7 %collective-permute-start.1 = (bf16[16,1024]{1,0:T(8,128)(2,1)S(1)}, bf16[16,1024]{1,0:T(8,128)(2,1)S(1)}, u32[]{:S(2)}, u32[]{:S(2)}) collective-permute-start(bf16[16,1024]{1,0:T(8,128)(2,1)S(1)} %collective-permute-done), channel_id=1, source_target_pairs={{0,1},{1,2},{2,3},{3,0},{4,5},{5,6},{6,7},{7,4},{8,9},{9,10},{10,1... | collective-permute-start | bytes 98312 | tf_op jit(solution)/shard_map/ppermute | solution.py:32
  20.1 5.7 %collective-permute-start.2 = (bf16[16,1024]{1,0:T(8,128)(2,1)S(1)}, bf16[16,1024]{1,0:T(8,128)(2,1)S(1)}, u32[]{:S(2)}, u32[]{:S(2)}) collective-permute-start(bf16[16,1024]{1,0:T(8,128)(2,1)S(1)} %collective-permute-done.1), channel_id=1, source_target_pairs={{0,1},{1,2},{2,3},{3,0},{4,5},{5,6},{6,7},{7,4},{8,9},{9,10},{10,1... | collective-permute-start | bytes 98312 | tf_op jit(solution)/shard_map/ppermute | solution.py:32
  28.4 24.4 %all-to-all-start = ((bf16[8,16,4096]{2,1,0:T(8,128)(2,1)}), bf16[8,16,4096]{2,1,0:T(8,128)(2,1)S(1)}, u32[]{:S(2)}, u32[]{:S(2)}) async-start(bf16[8,16,4096]{2,1,0:T(8,128)(2,1)} %convolution_convert_fusion.2), calls=%async_computation | async-start | bytes 2097152 | tf_op jit(solution)/shard_map/all_to_all | solution.py:36
  32.3 5.9 %collective-permute-start.3 = (bf16[16,1024]{1,0:T(8,128)(2,1)}, bf16[16,1024]{1,0:T(8,128)(2,1)S(1)}, u32[]{:S(2)}, u32[]{:S(2)}) collective-permute-start(bf16[16,1024]{1,0:T(8,128)(2,1)} %param.15), channel_id=1, source_target_pairs={{0,1},{1,2},{2,3},{3,0},{4,5},{5,6},{6,7},{7,4},{8,9},{9,10},{10,1... | collective-permute-start | bytes 98312 | tf_op jit(solution)/shard_map/ppermute | solution.py:32
  38.2 5.7 %collective-permute-start.4 = (bf16[16,1024]{1,0:T(8,128)(2,1)S(1)}, bf16[16,1024]{1,0:T(8,128)(2,1)S(1)}, u32[]{:S(2)}, u32[]{:S(2)}) collective-permute-start(bf16[16,1024]{1,0:T(8,128)(2,1)S(1)} %collective-permute-done.3), channel_id=1, source_target_pairs={{0,1},{1,2},{2,3},{3,0},{4,5},{5,6},{6,7},{7,4},{8,9},{9,10},{10,1... | collective-permute-start | bytes 98312 | tf_op jit(solution)/shard_map/ppermute | solution.py:32
  43.9 5.7 %collective-permute-start.5 = (bf16[16,1024]{1,0:T(8,128)(2,1)S(1)}, bf16[16,1024]{1,0:T(8,128)(2,1)S(1)}, u32[]{:S(2)}, u32[]{:S(2)}) collective-permute-start(bf16[16,1024]{1,0:T(8,128)(2,1)S(1)} %collective-permute-done.4), channel_id=1, source_target_pairs={{0,1},{1,2},{2,3},{3,0},{4,5},{5,6},{6,7},{7,4},{8,9},{9,10},{10,1... | collective-permute-start | bytes 98312 | tf_op jit(solution)/shard_map/ppermute | solution.py:32
  52.8 19.6 %all-to-all-start.2 = ((bf16[8,16,4096]{2,1,0:T(8,128)(2,1)}), bf16[8,16,4096]{2,1,0:T(8,128)(2,1)S(1)}, u32[]{:S(2)}, u32[]{:S(2)}) async-start(bf16[8,16,4096]{2,1,0:T(8,128)(2,1)} %convolution_convert_fusion), calls=%async_computation.3 | async-start | bytes 2097152 | tf_op jit(solution)/shard_map/all_to_all | solution.py:36
  57.0 33.4 %reduce-scatter.3.cloned.1.call-start = ((), (), s32[]{:S(2)}) async-start(), calls=%async_computation.6 | async-start | bytes 1310720 | tf_op jit(solution)/shard_map/reduce_scatter | solution.py:41
  57.0 3.5 %copy-start.2 = (bf16[1,4096,512]{2,1,0:T(8,128)(2,1)S(1)}, bf16[1,4096,512]{2,1,0:T(8,128)(2,1)}, u32[]{:S(2)}) copy-start(bf16[1,4096,512]{2,1,0:T(8,128)(2,1)} %param.13) | copy-start | bytes 12582916
  60.5 2.2 %copy-start = (bf16[1,512,4096]{2,1,0:T(8,128)(2,1)S(1)}, bf16[1,512,4096]{2,1,0:T(8,128)(2,1)}, u32[]{:S(2)}) copy-start(bf16[1,512,4096]{2,1,0:T(8,128)(2,1)} %param.14) | copy-start | bytes 12582916
  64.4 54.1 %reduce-scatter.5.cloned.1.call-start = ((), (), s32[]{:S(2)}) async-start(), calls=%async_computation.7 | async-start | bytes 1310720 | tf_op jit(solution)/shard_map/reduce_scatter | solution.py:41
  72.4 3.9 %copy-start.1 = (bf16[1,4096,512]{2,1,0:T(8,128)(2,1)S(1)}, bf16[1,4096,512]{2,1,0:T(8,128)(2,1)}, u32[]{:S(2)}) copy-start(bf16[1,4096,512]{2,1,0:T(8,128)(2,1)} %param.12) | copy-start | bytes 12582916
  76.3 2.2 %copy-start.3 = (bf16[1,4096,512]{2,1,0:T(8,128)(2,1)S(1)}, bf16[1,4096,512]{2,1,0:T(8,128)(2,1)}, u32[]{:S(2)}) copy-start(bf16[1,4096,512]{2,1,0:T(8,128)(2,1)} %param.13) | copy-start | bytes 12582916
  90.4 28.2 %all-to-all-start.1 = ((bf16[8,16,1024]{2,1,0:T(8,128)(2,1)}), bf16[8,16,1024]{2,1,0:T(8,128)(2,1)S(1)}, u32[]{:S(2)}, u32[]{:S(2)}) async-start(bf16[8,16,1024]{2,1,0:T(8,128)(2,1)} %reduce-scatter.3.cloned.1.call-done), calls=%async_computation.2 | async-start | bytes 524288 | tf_op jit(solution)/shard_map/all_to_all | solution.py:44
  118.6 10.6 %all-to-all-start.3 = ((bf16[8,16,1024]{2,1,0:T(8,128)(2,1)}), bf16[8,16,1024]{2,1,0:T(8,128)(2,1)S(1)}, u32[]{:S(2)}, u32[]{:S(2)}) async-start(bf16[8,16,1024]{2,1,0:T(8,128)(2,1)} %reduce-scatter.5.cloned.1.call-done), calls=%async_computation.5 | async-start | bytes 524288 | tf_op jit(solution)/shard_map/all_to_all | solution.py:44
Sparse Core Ops, SparseCore 0:
  64.6 25.7 reduce-scatter.2
  92.8 25.7 reduce-scatter.4
